TPU v7x, 128 devices: a whole 4x4x4 slice. The times are simulated.
128 devices in a mesh: row: 8 (over y, core), col: 16 (over z, x).
Axes of the slice: x: 4, y: 4, z: 4, core: 2. Of those that a mesh axis runs over, the one named last changes fastest.
Arguments:
- block_x: float32 [64, 98304], P(None, ('row', 'col')), may hold values from -6 to 6
- block_p: float32 [64, 98304], P(None, ('row', 'col')), may hold values from -6 to 6
- tile_rows: int32 [8, 16, 576], P('row', 'col'), may hold values from 0 to 95, as said below
- tile_cols: int32 [8, 16, 576], P('row', 'col'), may hold values from 0 to 47, as said below
- tile_count: int32 [8, 16], P('row', 'col'), may hold values from 1 to 576, as said below
- tile_vals: bfloat16 [8, 16, 576, 128, 128], P('row', 'col'), may hold values from -0.125 to 0.125
Outputs:
- residual: float32 [64, 98304], P(None, ('row', 'col'))
- image_r: float32 [64, 98304], P(None, ('row', 'col'))
- gram_a: float32 [192, 192], replicated
- gram_b: float32 [192, 192], replicated
Inputs may be any that keep to these rules, and one draw needn't show every extreme that they name: `tile_rows`: within one grid cell the live slots name distinct tiles, all with i <= j; slots at and beyond the cell's count are ignored. `tile_cols`: paired with tile_rows slot by slot. `tile_count`: some grid cell is full in every draw.
All inputs are finite; a program needn't handle non-finite values.
Results may differ from a plain program's by a relative error of at most 0.0035.
Values may be sent and summed in bfloat16 or wider, within the bound.
A program may use at most 128 MiB of HBM per device.

v0:
```python
import math
import jax
import jax.numpy as jnp
from jax import lax
from jax.sharding import PartitionSpec as P


def apply_graph(vectors, tile_rows, tile_cols, live_count, tile_vals):
    vec_width = vectors.shape[0]
    tile_size = tile_vals.shape[-1]
    row_range = lax.all_gather(vectors, "col", axis=1, tiled=True)
    col_group = lax.all_gather(vectors, "row", axis=1, tiled=True)
    row_blocks = row_range.reshape(vec_width, -1, tile_size)
    col_blocks = col_group.reshape(vec_width, -1, tile_size)
    group_size = math.gcd(tile_vals.shape[0], 64)
    offsets = jnp.arange(group_size, dtype=jnp.int32)
    turn_count = (live_count + group_size - 1) // group_size

    def slot_group(turn_index):
        first_slot = turn_index * group_size
        row_index = lax.dynamic_slice_in_dim(tile_rows, first_slot, group_size)
        col_index = lax.dynamic_slice_in_dim(tile_cols, first_slot, group_size)
        values = lax.dynamic_slice_in_dim(tile_vals, first_slot, group_size, 0)
        live_slots = first_slot + offsets < live_count
        return (row_index, col_index, values, live_slots)

    def turn(turn_index, totals):
        row_totals, col_totals = totals
        row_index, col_index, values, live_slots = slot_group(turn_index)
        values = jnp.where(live_slots[:, None, None], values, jnp.zeros_like(values))
        col_inputs = jnp.take(col_blocks, col_index, axis=1)
        row_inputs = jnp.take(row_blocks, row_index, axis=1)
        forward = jnp.einsum("wgb,gab->wga", col_inputs, values, preferred_element_type=jnp.float32)
        backward = jnp.einsum(
            "wga,gab->wgb", row_inputs, values, preferred_element_type=jnp.float32
        )
        return (row_totals.at[:, row_index].add(forward), col_totals.at[:, col_index].add(backward))

    start_rows = jnp.zeros(row_blocks.shape, jnp.float32)
    start_cols = jnp.zeros(col_blocks.shape, jnp.float32)
    row_totals, col_totals = lax.fori_loop(0, turn_count, turn, (start_rows, start_cols))
    own_rows = lax.psum_scatter(
        row_totals.reshape(vec_width, -1), "col", scatter_dimension=1, tiled=True
    )
    own_cols = lax.psum_scatter(
        col_totals.reshape(vec_width, -1), "row", scatter_dimension=1, tiled=True
    )
    return own_rows + own_cols


def per_device(block_x, block_p, tile_rows, tile_cols, tile_count, tile_vals):
    highest = lax.Precision.HIGHEST
    width_k = block_x.shape[0]
    node_count = block_x.shape[1] * lax.axis_size("row") * lax.axis_size("col")
    slot_rows = tile_rows[0, 0]
    slot_cols = tile_cols[0, 0]
    live_count = tile_count[0, 0]
    slot_vals = tile_vals[0, 0]

    def product(left, right):
        return (
            jnp.dot(left, right.T, precision=highest, preferred_element_type=jnp.float32)
            / node_count
        )

    gram_x = lax.psum(product(block_x, block_x), ("row", "col"))
    cholesky_factor = jnp.linalg.cholesky(gram_x)
    orthonormal = lax.linalg.triangular_solve(cholesky_factor, block_x, left_side=True, lower=True)
    ortho_low = orthonormal.astype(jnp.bfloat16)
    dir_low = block_p.astype(jnp.bfloat16)
    both_images = apply_graph(
        jnp.concatenate([ortho_low, dir_low], axis=0), slot_rows, slot_cols, live_count, slot_vals
    )
    image_x = both_images[:width_k]
    image_p = both_images[width_k:]
    rayleigh = lax.psum(product(orthonormal, image_x), ("row", "col"))
    residual = image_x - jnp.dot(
        rayleigh.T, orthonormal, precision=highest, preferred_element_type=jnp.float32
    )
    residual_low = residual.astype(jnp.bfloat16)
    image_r = apply_graph(residual_low, slot_rows, slot_cols, live_count, slot_vals)
    basis = jnp.concatenate([orthonormal, residual, block_p], axis=0)
    images = jnp.concatenate([image_x, image_r, image_p], axis=0)
    gram_a, gram_b = lax.psum((product(basis, images), product(basis, basis)), ("row", "col"))
    return (residual, image_r, gram_a, gram_b)


def solution(mesh):
    in_specs = (
        P(None, ("row", "col")),
        P(None, ("row", "col")),
        P("row", "col", None),
        P("row", "col", None),
        P("row", "col"),
        P("row", "col", None, None, None),
    )
    out_specs = (P(None, ("row", "col")), P(None, ("row", "col")), P(), P())
    return jax.shard_map(
        per_device, mesh=mesh, in_specs=in_specs, out_specs=out_specs, check_vma=False
    )
```

profile of v0, /device:TPU:1, one launch (start us, length us, event | category | flops | bytes accessed | tf_op | source)
XLA Modules:
  0.0 1301.9 jit_solution(9293041823528149920)
XLA Ops:
  8.4 68.9 %psum.28 = f32[64,64]{0,1:T(8,128)S(1)} all-reduce(f32[64,64]{0,1:T(8,128)S(1)} %convolution_multiply_fusion.3), channel_id=1, replica_groups=mesh['row'=8,'col'=16] {'row','col'}, use_global_device_ids=true, to_apply=%region_0.0 | all-reduce | flops 4096 | bytes 32768 | tf_op jit(solution)/shard_map/psum | solution.py:66
  77.4 5.8 cholesky.16
  84.6 4.9 custom-call.6
  93.1 19.8 %all-gather.4.cloned.1.call-done = bf16[128,6144]{1,0:T(8,128)(2,1)} async-done(((bf16[128,768]{1,0:T(8,128)(2,1)}), bf16[128,6144]{1,0:T(8,128)(2,1)}) %all-gather.4.cloned.1.call-update) | async-done | bytes 1572880 | tf_op jit(solution)/shard_map/all_gather | solution.py:12
  115.9 47.5 %all-gather.6.cloned.1.call-done = bf16[128,12288]{1,0:T(8,128)(2,1)} async-done(((bf16[128,768]{1,0:T(8,128)(2,1)}), bf16[128,12288]{1,0:T(8,128)(2,1)}) %all-gather.6.cloned.1.call-update) | async-done | bytes 3145744 | tf_op jit(solution)/shard_map/all_gather | solution.py:11
  163.3 4.5 copy_bitcast_fusion.3
  171.6 290.6 %while.26 = (s32[]{:T(128)}, f32[128,96,128]{2,0,1:T(8,128)}, f32[128,48,128]{2,0,1:T(8,128)S(1)}, s32[]{:T(128)}, s32[576]{0:T(1024)S(1)}, /*index=5*/s32[]{:T(...) while((s32[]{:T(128)}, f32[128,96,128]{2,0,1:T(8,128)}, ...), condition=%wide.region_6.7_spmd.clone, body=%wide.region_3.6_spmd.clone.sunk | while | flops 543165312 | bytes 50343056 | solution.py:41
  175.9 5.8 fusion.80
  181.7 13.6 %scatter_fusion = f32[128,96,128]{2,0,1:T(8,128)} fusion(f32[128,96,128]{2,0,1:T(8,128)} %get-tuple-element.407, s32[64]{0:T(128)S(1)} %get-tuple-element.374, f32[64,128,128]{2,1,0:T(8,128)} %fusion.80), kind=kCustom, calls=%fused_computation.4.clone.clone.1 | custom fusion | flops 1048576 | bytes 12583168 | tf_op jit(solution)/shard_map/while/body/scatter-add | solution.py:37
  195.4 4.0 gather_fusion.1
  199.4 4.9 fusion.81
  204.3 8.8 scatter_fusion.1
  217.4 5.8 fusion.80
  223.2 13.6 %scatter_fusion = f32[128,96,128]{2,0,1:T(8,128)} fusion(f32[128,96,128]{2,0,1:T(8,128)} %get-tuple-element.407, s32[64]{0:T(128)S(1)} %get-tuple-element.374, f32[64,128,128]{2,1,0:T(8,128)} %fusion.80), kind=kCustom, calls=%fused_computation.4.clone.clone.1 | custom fusion | flops 1048576 | bytes 12583168 | tf_op jit(solution)/shard_map/while/body/scatter-add | solution.py:37
  236.9 4.0 gather_fusion.1
  240.9 4.9 fusion.81
  245.8 8.8 scatter_fusion.1
  258.9 5.8 fusion.80
  264.8 13.6 %scatter_fusion = f32[128,96,128]{2,0,1:T(8,128)} fusion(f32[128,96,128]{2,0,1:T(8,128)} %get-tuple-element.407, s32[64]{0:T(128)S(1)} %get-tuple-element.374, f32[64,128,128]{2,1,0:T(8,128)} %fusion.80), kind=kCustom, calls=%fused_computation.4.clone.clone.1 | custom fusion | flops 1048576 | bytes 12583168 | tf_op jit(solution)/shard_map/while/body/scatter-add | solution.py:37
  278.4 4.0 gather_fusion.1
  282.4 4.9 fusion.81
  287.3 8.8 scatter_fusion.1
  300.5 5.8 fusion.80
  306.3 13.5 %scatter_fusion = f32[128,96,128]{2,0,1:T(8,128)} fusion(f32[128,96,128]{2,0,1:T(8,128)} %get-tuple-element.407, s32[64]{0:T(128)S(1)} %get-tuple-element.374, f32[64,128,128]{2,1,0:T(8,128)} %fusion.80), kind=kCustom, calls=%fused_computation.4.clone.clone.1 | custom fusion | flops 1048576 | bytes 12583168 | tf_op jit(solution)/shard_map/while/body/scatter-add | solution.py:37
  319.8 4.0 gather_fusion.1
  323.9 4.9 fusion.81
  328.8 8.8 scatter_fusion.1
  341.9 5.8 fusion.80
  347.7 13.6 %scatter_fusion = f32[128,96,128]{2,0,1:T(8,128)} fusion(f32[128,96,128]{2,0,1:T(8,128)} %get-tuple-element.407, s32[64]{0:T(128)S(1)} %get-tuple-element.374, f32[64,128,128]{2,1,0:T(8,128)} %fusion.80), kind=kCustom, calls=%fused_computation.4.clone.clone.1 | custom fusion | flops 1048576 | bytes 12583168 | tf_op jit(solution)/shard_map/while/body/scatter-add | solution.py:37
  361.3 4.0 gather_fusion.1
  365.4 4.9 fusion.81
  370.3 8.8 scatter_fusion.1
  383.4 5.8 fusion.80
  389.2 13.6 %scatter_fusion = f32[128,96,128]{2,0,1:T(8,128)} fusion(f32[128,96,128]{2,0,1:T(8,128)} %get-tuple-element.407, s32[64]{0:T(128)S(1)} %get-tuple-element.374, f32[64,128,128]{2,1,0:T(8,128)} %fusion.80), kind=kCustom, calls=%fused_computation.4.clone.clone.1 | custom fusion | flops 1048576 | bytes 12583168 | tf_op jit(solution)/shard_map/while/body/scatter-add | solution.py:37
  406.9 4.9 fusion.81
  411.8 8.8 scatter_fusion.1
  424.9 5.8 fusion.80
  430.7 13.6 %scatter_fusion = f32[128,96,128]{2,0,1:T(8,128)} fusion(f32[128,96,128]{2,0,1:T(8,128)} %get-tuple-element.407, s32[64]{0:T(128)S(1)} %get-tuple-element.374, f32[64,128,128]{2,1,0:T(8,128)} %fusion.80), kind=kCustom, calls=%fused_computation.4.clone.clone.1 | custom fusion | flops 1048576 | bytes 12583168 | tf_op jit(solution)/shard_map/while/body/scatter-add | solution.py:37
  448.4 4.9 fusion.81
  453.3 8.8 scatter_fusion.1
  464.2 6.1 copy_bitcast_fusion
  470.4 106.4 %reduce-scatter.7.cloned.1.call-done = f32[128,768]{1,0:T(8,128)} async-done(((f32[128,6144]{1,0:T(8,128)}), f32[128,768]{1,0:T(8,128)}) %reduce-scatter.7.cloned.1.call-update) | async-done | bytes 393232 | tf_op jit(solution)/shard_map/reduce_scatter | solution.py:45
  576.8 85.4 %reduce-scatter.5.cloned.1.call-done = f32[128,768]{1,0:T(8,128)} async-done(((f32[128,12288]{1,0:T(8,128)}), f32[128,768]{1,0:T(8,128)}) %reduce-scatter.5.cloned.1.call-update) | async-done | bytes 393232 | tf_op jit(solution)/shard_map/reduce_scatter | solution.py:42
  663.6 65.7 %psum.29 = f32[64,64]{0,1:T(8,128)S(1)} all-reduce(f32[64,64]{0,1:T(8,128)S(1)} %convolution_multiply_fusion.2), channel_id=1, replica_groups=mesh['row'=8,'col'=16] {'row','col'}, use_global_device_ids=true, to_apply=%region_9.10 | all-reduce | flops 4096 | bytes 32768 | tf_op jit(solution)/shard_map/psum | solution.py:76
  730.4 14.3 %all_gather.14 = bf16[64,6144]{1,0:T(8,128)(2,1)S(1)} all-gather(bf16[64,768]{1,0:T(8,128)(2,1)} %get-tuple-element.250), channel_id=1, replica_groups=mesh['row'=8,'col'=16] {'row'}, dimensions={1}, use_global_device_ids=true | all-gather | bytes 884736 | tf_op jit(solution)/shard_map/all_gather | solution.py:12
  745.8 24.0 %all-gather.8.cloned.1.call-done = bf16[64,12288]{1,0:T(8,128)(2,1)} async-done(((bf16[64,768]{1,0:T(8,128)(2,1)}), bf16[64,12288]{1,0:T(8,128)(2,1)}) %all-gather.8.cloned.1.call-update) | async-done | bytes 1572880 | tf_op jit(solution)/shard_map/all_gather | solution.py:11
  776.2 198.4 %while.27 = (s32[]{:T(128)}, f32[64,96,128]{2,0,1:T(8,128)}, f32[64,48,128]{2,0,1:T(8,128)}, s32[]{:T(128)}, s32[576]{0:T(1024)S(1)}, /*index=5*/s32[]{:T(128)},...) while((s32[]{:T(128)}, f32[64,96,128]{2,0,1:T(8,128)}, ...), condition=%wide.region_13.14_spmd.clone, body=%wide.region_10.13_spmd.clone.sunk | while | flops 272632704 | bytes 27274384 | solution.py:41
  782.0 9.0 scatter_fusion.2
  795.5 9.0 scatter_fusion.3
  810.4 9.0 scatter_fusion.2
  823.9 9.0 scatter_fusion.3
  838.7 9.0 scatter_fusion.2
  852.2 9.0 scatter_fusion.3
  867.0 9.0 scatter_fusion.2
  880.5 9.0 scatter_fusion.3
  895.3 9.0 scatter_fusion.2
  908.9 9.0 scatter_fusion.3
  923.6 9.1 scatter_fusion.2
  937.2 9.0 scatter_fusion.3
  952.0 9.0 scatter_fusion.2
  965.5 9.0 scatter_fusion.3
  981.7 80.2 %reduce-scatter.11.cloned.1.call-done = f32[64,768]{1,0:T(8,128)} async-done(((f32[64,6144]{1,0:T(8,128)}), f32[64,768]{1,0:T(8,128)}) %reduce-scatter.11.cloned.1.call-update) | async-done | bytes 196624 | tf_op jit(solution)/shard_map/reduce_scatter | solution.py:45
  1061.9 79.4 %reduce-scatter.9.cloned.1.call-done = f32[64,768]{1,0:T(8,128)} async-done(((f32[64,12288]{1,0:T(8,128)}), f32[64,768]{1,0:T(8,128)}) %reduce-scatter.9.cloned.1.call-update) | async-done | bytes 196624 | tf_op jit(solution)/shard_map/reduce_scatter | solution.py:42
  1143.7 148.1 %all-reduce.3.cloned.1.call-done = (f32[192,192]{1,0:T(8,128)}, f32[192,192]{1,0:T(8,128)}) async-done(((f32[192,192]{1,0:T(8,128)}, f32[192,192]{1,0:T(8,128)}), (f32[192,192]{1,0:T(8,128)}, f32[192,192]{1,0:T(8,128)})) %all-reduce.3.cloned.1.call-update) | async-done | bytes 294928 | tf_op jit(solution)/shard_map/psum | solution.py:84
  (159 shorter events, 147.3 us)
Async XLA Ops:
  7.2 0.9 copy-start
  7.2 85.8 %copy-start.8 = (s32[1,1,576]{2,1,0:T(1,128)S(1)}, s32[1,1,576]{2,1,0:T(1,128)}, u32[]{:S(2)}) copy-start(s32[1,1,576]{2,1,0:T(1,128)} %param.12) | copy-start | bytes 6916
  7.2 85.8 %copy-start.9 = (s32[1,1,576]{2,1,0:T(1,128)S(1)}, s32[1,1,576]{2,1,0:T(1,128)}, u32[]{:S(2)}) copy-start(s32[1,1,576]{2,1,0:T(1,128)} %param.13) | copy-start | bytes 6916
  7.2 105.7 %all-gather.4.cloned.1.call-start = ((), (), s32[]{:S(2)}) async-start(), calls=%async_computation.4 | async-start | bytes 1769472 | tf_op jit(solution)/shard_map/all_gather | solution.py:12
  91.5 71.8 %all-gather.6.cloned.1.call-start = ((), (), s32[]{:S(2)}) async-start(), calls=%async_computation.5 | async-start | bytes 3342336 | tf_op jit(solution)/shard_map/all_gather | solution.py:11
  92.3 484.5 %reduce-scatter.7.cloned.1.call-start = ((), (), s32[]{:S(2)}) async-start(), calls=%async_computation.7 | async-start | bytes 3538944 | tf_op jit(solution)/shard_map/reduce_scatter | solution.py:45
  464.2 198.0 %reduce-scatter.5.cloned.1.call-start = ((), (), s32[]{:S(2)}) async-start(), calls=%async_computation.6 | async-start | bytes 6684672 | tf_op jit(solution)/shard_map/reduce_scatter | solution.py:42
  470.3 299.4 %all-gather.8.cloned.1.call-start = ((), (), s32[]{:S(2)}) async-start(), calls=%async_computation.8 | async-start | bytes 1671168 | tf_op jit(solution)/shard_map/all_gather | solution.py:11
  663.3 109.5 %copy-start.3 = (f32[128,768]{1,0:T(8,128)}, f32[128,768]{1,0:T(8,128)S(1)}, u32[]{:S(2)}) copy-start(f32[128,768]{1,0:T(8,128)S(1)} %add.116) | copy-start | bytes 1179652
  730.3 331.6 %reduce-scatter.11.cloned.1.call-start = ((), (), s32[]{:S(2)}) async-start(), calls=%async_computation.10 | async-start | bytes 1769472 | tf_op jit(solution)/shard_map/reduce_scatter | solution.py:45
  974.6 2.9 copy-start.2
  977.4 163.9 %reduce-scatter.9.cloned.1.call-start = ((), (), s32[]{:S(2)}) async-start(), calls=%async_computation.9 | async-start | bytes 3342336 | tf_op jit(solution)/shard_map/reduce_scatter | solution.py:42
  979.3 0.9 copy-start.5
  979.3 1.0 copy-start.6
  979.3 2.3 copy-start.4
  979.3 312.4 %all-reduce.3.cloned.1.call-start = ((), (), s32[]{:S(2)}) async-start(), calls=%async_computation.11 | async-start | bytes 786432 | tf_op jit(solution)/shard_map/psum | solution.py:84
  980.3 314.7 %copy-start.1 = (f32[64,768]{1,0:T(8,128)S(1)}, f32[64,768]{1,0:T(8,128)}, u32[]{:S(2)}) copy-start(f32[64,768]{1,0:T(8,128)} %param.10) | copy-start | bytes 589828
  1142.3 152.7 %copy-start.7 = (f32[64,768]{1,0:T(8,128)}, f32[64,768]{1,0:T(8,128)S(1)}, u32[]{:S(2)}) copy-start(f32[64,768]{1,0:T(8,128)S(1)} %add.117) | copy-start | bytes 589828
Sparse Core Ops, SparseCore 0:
  91.7 21.1 all-gather.3
  115.6 47.6 all-gather.5
  464.3 112.4 reduce-scatter.6
  580.0 82.0 reduce-scatter.4
  730.4 39.2 all-gather.7
  977.5 84.3 reduce-scatter.10
  1065.2 76.0 reduce-scatter.8
  1146.6 145.1 all-reduce.2
where the time goes:
time: 1310 us; the launch traced here: 1300 us
  waiting for transfers between devices  591 us (45%)
  other arithmetic  309 us (24%)
  blocking collectives  149 us (11%)
  local copies, waits for them, and re-layouts  118 us (9%)
  matrix products  118 us (9%)
  between operations  15 us (1%)
    reduce_scatter x2, waiting for transfers between devices, apply_graph(): lax.psum_scatter(col_totals.reshape(vec_width, -1), 'row', scatter_dimens...  187 us
    reduce_scatter x2, waiting for transfers between devices, apply_graph(): lax.psum_scatter(row_totals.reshape(vec_width, -1), 'col', scatter_dimens...  165 us
    scatter-add x14, other arithmetic, turn(): row_totals.at[:, row_index].add(forward)  158 us
    psum x1, waiting for transfers between devices, per_device(): lax.psum((product(basis, images), product(basis, basis)), ('row', 'col'))  148 us
    scatter-add x14, other arithmetic, turn(): col_totals.at[:, col_index].add(backward)  125 us
    all_gather x2, waiting for transfers between devices, apply_graph(): row_range = lax.all_gather(vectors, 'col', axis=1, tiled=True)  71.4 us
    psum x1, blocking collectives, per_device(): gram_x = lax.psum(product(block_x, block_x), ('row', 'col'))  68.9 us
    psum x1, blocking collectives, per_device(): rayleigh = lax.psum(product(orthonormal, image_x), ('row', 'col'))  65.7 us
  transfers between devices with their start and end apart: 8, of which 8 were waited for; matrix products, arithmetic and copies ran while one was open for 1% of the time, Pallas kernels for 0%

commit v1 on v0

--- a/solution.py
+++ b/solution.py
@@ -8,7 +8,17 @@
 def apply_graph(vectors, tile_rows, tile_cols, live_count, tile_vals):
     vec_width = vectors.shape[0]
     tile_size = tile_vals.shape[-1]
-    row_range = lax.all_gather(vectors, "col", axis=1, tiled=True)
+    current_arr = lax.axis_size("col")
+    val = lax.axis_index("col")
+    step_out, x_new = (current_arr, val)
+    row_range, m_next = (vectors, 1)
+    while m_next < step_out:
+        carry_in = tuple(((t, t ^ m_next) for t in range(step_out)))
+        block_last = lax.ppermute(row_range, axis_name="col", perm=carry_in)
+        block_next = jnp.concatenate([row_range, block_last], axis=1)
+        new = jnp.concatenate([block_last, row_range], axis=1)
+        row_range = jnp.where(x_new & m_next == 0, block_next, new)
+        m_next = 2 * m_next
     col_group = lax.all_gather(vectors, "row", axis=1, tiled=True)
     row_blocks = row_range.reshape(vec_width, -1, tile_size)
     col_blocks = col_group.reshape(vec_width, -1, tile_size)

time: 1310 us -> 1320 us (level)
  waiting for transfers between devices: 591 us -> 576 us
    all_gather x2 -> x0, waiting for transfers between devices: 71.4 us -> none  [apply_graph(): row_range = lax.all_gather(vectors, 'col', axis=1, tiled=True)]
    ppermute x0 -> x8, waiting for transfers between devices: none -> 70.7 us  [apply_graph(): block_last = lax.ppermute(row_range, axis_name='col', perm=carry_in)]
    all_gather x1, waiting for transfers between devices: 19.8 us -> 2.81 us  [apply_graph(): col_group = lax.all_gather(vectors, 'row', axis=1, tiled=True)]
  transfers between devices with their start and end apart: 8 -> 14, of which waited for: 8 -> 13; matrix products, arithmetic and copies ran while one was open for 1% -> 1% of each run, Pallas kernels for 0% -> 0%
where the time goes in v1:
time: 1320 us; the launch traced here: 1310 us
  waiting for transfers between devices  576 us (44%)
  other arithmetic  319 us (24%)
  blocking collectives  152 us (12%)
  local copies, waits for them, and re-layouts  120 us (9%)
  matrix products  118 us (9%)
  between operations  15.2 us (1%)
    reduce_scatter x2, waiting for transfers between devices, apply_graph(): lax.psum_scatter(col_totals.reshape(vec_width, -1), 'row', scatter_dimens...  189 us
    reduce_scatter x2, waiting for transfers between devices, apply_graph(): lax.psum_scatter(row_totals.reshape(vec_width, -1), 'col', scatter_dimens...  165 us
    scatter-add x14, other arithmetic, turn(): row_totals.at[:, row_index].add(forward)  160 us
    psum x1, waiting for transfers between devices, per_device(): lax.psum((product(basis, images), product(basis, basis)), ('row', 'col'))  148 us
    scatter-add x14, other arithmetic, turn(): col_totals.at[:, col_index].add(backward)  125 us
    ppermute x8, waiting for transfers between devices, apply_graph(): block_last = lax.ppermute(row_range, axis_name='col', perm=carry_in)  70.7 us
    psum x1, blocking collectives, per_device(): gram_x = lax.psum(product(block_x, block_x), ('row', 'col'))  68.9 us
    psum x1, blocking collectives, per_device(): rayleigh = lax.psum(product(orthonormal, image_x), ('row', 'col'))  65.5 us
  transfers between devices with their start and end apart: 14, of which 13 were waited for; matrix products, arithmetic and copies ran while one was open for 1% of the time, Pallas kernels for 0%

profile of v1, /device:TPU:1, one launch (start us, length us, event | category | flops | bytes accessed | tf_op | source)
XLA Modules:
  0.0 1306.1 jit_solution(6382954447680194586)
XLA Ops:
  8.4 68.9 %psum.28 = f32[64,64]{0,1:T(8,128)S(1)} all-reduce(f32[64,64]{0,1:T(8,128)S(1)} %convolution_multiply_fusion.3), channel_id=1, replica_groups=mesh['row'=8,'col'=16] {'row','col'}, use_global_device_ids=true, to_apply=%region_0.0 | all-reduce | flops 4096 | bytes 32768 | tf_op jit(solution)/shard_map/psum | solution.py:76
  77.4 5.8 cholesky.16
  84.6 4.9 custom-call.6
  91.0 5.5 collective-permute-done
  97.9 9.2 collective-permute-done.1
  107.4 16.2 %collective-permute-done.2 = bf16[128,3072]{1,0:T(8,128)(2,1)S(1)} collective-permute-done((bf16[128,3072]{1,0:T(8,128)(2,1)S(1)}, bf16[128,3072]{1,0:T(8,128)(2,1)S(1)}, u32[]{:S(2)}, u32[]{:S(2)}) %collective-permute-start.2) | collective-permute-done | bytes 786464 | tf_op jit(solution)/shard_map/ppermute | solution.py:17
  135.3 24.0 %collective-permute-done.3 = bf16[128,6144]{1,0:T(8,128)(2,1)} collective-permute-done((bf16[128,6144]{1,0:T(8,128)(2,1)}, bf16[128,6144]{1,0:T(8,128)(2,1)}, u32[]{:S(2)}, u32[]{:S(2)}) %collective-permute-start.3) | collective-permute-done | bytes 1572896 | tf_op jit(solution)/shard_map/ppermute | solution.py:17
  171.7 291.1 %while.26 = (s32[]{:T(128)}, f32[128,96,128]{2,0,1:T(8,128)}, f32[128,48,128]{2,0,1:T(8,128)S(1)}, s32[]{:T(128)}, s32[576]{0:T(1024)S(1)}, /*index=5*/s32[]{:T(...) while((s32[]{:T(128)}, f32[128,96,128]{2,0,1:T(8,128)}, ...), condition=%wide.region_6.7_spmd.clone, body=%wide.region_3.6_spmd.clone.sunk | while | flops 543165312 | bytes 50343056 | solution.py:51
  176.2 5.8 fusion.78
  182.0 13.7 %scatter_fusion = f32[128,96,128]{2,0,1:T(8,128)} fusion(f32[128,96,128]{2,0,1:T(8,128)} %get-tuple-element.407, s32[64]{0:T(128)S(1)} %get-tuple-element.374, f32[64,128,128]{2,1,0:T(8,128)} %fusion.78), kind=kCustom, calls=%fused_computation.4.clone.clone.1 | custom fusion | flops 1048576 | bytes 12583168 | tf_op jit(solution)/shard_map/while/body/scatter-add | solution.py:47
  195.7 4.0 gather_fusion.1
  199.7 4.9 fusion.79
  204.6 8.8 scatter_fusion.1
  217.7 5.8 fusion.78
  223.6 13.7 %scatter_fusion = f32[128,96,128]{2,0,1:T(8,128)} fusion(f32[128,96,128]{2,0,1:T(8,128)} %get-tuple-element.407, s32[64]{0:T(128)S(1)} %get-tuple-element.374, f32[64,128,128]{2,1,0:T(8,128)} %fusion.78), kind=kCustom, calls=%fused_computation.4.clone.clone.1 | custom fusion | flops 1048576 | bytes 12583168 | tf_op jit(solution)/shard_map/while/body/scatter-add | solution.py:47
  241.3 4.9 fusion.79
  246.2 8.8 scatter_fusion.1
  259.3 5.8 fusion.78
  265.1 13.7 %scatter_fusion = f32[128,96,128]{2,0,1:T(8,128)} fusion(f32[128,96,128]{2,0,1:T(8,128)} %get-tuple-element.407, s32[64]{0:T(128)S(1)} %get-tuple-element.374, f32[64,128,128]{2,1,0:T(8,128)} %fusion.78), kind=kCustom, calls=%fused_computation.4.clone.clone.1 | custom fusion | flops 1048576 | bytes 12583168 | tf_op jit(solution)/shard_map/while/body/scatter-add | solution.py:47
  278.8 4.0 gather_fusion.1
  282.8 4.9 fusion.79
  287.8 8.8 scatter_fusion.1
  300.9 5.8 fusion.78
  306.7 13.6 %scatter_fusion = f32[128,96,128]{2,0,1:T(8,128)} fusion(f32[128,96,128]{2,0,1:T(8,128)} %get-tuple-element.407, s32[64]{0:T(128)S(1)} %get-tuple-element.374, f32[64,128,128]{2,1,0:T(8,128)} %fusion.78), kind=kCustom, calls=%fused_computation.4.clone.clone.1 | custom fusion | flops 1048576 | bytes 12583168 | tf_op jit(solution)/shard_map/while/body/scatter-add | solution.py:47
  320.3 4.0 gather_fusion.1
  324.3 4.9 fusion.79
  329.3 8.8 scatter_fusion.1
  342.4 5.8 fusion.78
  348.2 13.8 %scatter_fusion = f32[128,96,128]{2,0,1:T(8,128)} fusion(f32[128,96,128]{2,0,1:T(8,128)} %get-tuple-element.407, s32[64]{0:T(128)S(1)} %get-tuple-element.374, f32[64,128,128]{2,1,0:T(8,128)} %fusion.78), kind=kCustom, calls=%fused_computation.4.clone.clone.1 | custom fusion | flops 1048576 | bytes 12583168 | tf_op jit(solution)/shard_map/while/body/scatter-add | solution.py:47
  366.0 4.9 fusion.79
  370.9 8.8 scatter_fusion.1
  384.0 5.8 fusion.78
  389.9 13.7 %scatter_fusion = f32[128,96,128]{2,0,1:T(8,128)} fusion(f32[128,96,128]{2,0,1:T(8,128)} %get-tuple-element.407, s32[64]{0:T(128)S(1)} %get-tuple-element.374, f32[64,128,128]{2,1,0:T(8,128)} %fusion.78), kind=kCustom, calls=%fused_computation.4.clone.clone.1 | custom fusion | flops 1048576 | bytes 12583168 | tf_op jit(solution)/shard_map/while/body/scatter-add | solution.py:47
  407.5 4.9 fusion.79
  412.5 8.8 scatter_fusion.1
  425.6 5.8 fusion.78
  431.4 13.7 %scatter_fusion = f32[128,96,128]{2,0,1:T(8,128)} fusion(f32[128,96,128]{2,0,1:T(8,128)} %get-tuple-element.407, s32[64]{0:T(128)S(1)} %get-tuple-element.374, f32[64,128,128]{2,1,0:T(8,128)} %fusion.78), kind=kCustom, calls=%fused_computation.4.clone.clone.1 | custom fusion | flops 1048576 | bytes 12583168 | tf_op jit(solution)/shard_map/while/body/scatter-add | solution.py:47
  449.1 4.9 fusion.79
  454.0 8.8 scatter_fusion.1
  464.9 6.1 copy_bitcast_fusion
  471.0 110.2 %reduce-scatter.7.cloned.1.call-done = f32[128,768]{1,0:T(8,128)} async-done(((f32[128,6144]{1,0:T(8,128)}), f32[128,768]{1,0:T(8,128)}) %reduce-scatter.7.cloned.1.call-update) | async-done | bytes 393232 | tf_op jit(solution)/shard_map/reduce_scatter | solution.py:55
  581.2 85.7 %reduce-scatter.5.cloned.1.call-done = f32[128,768]{1,0:T(8,128)} async-done(((f32[128,12288]{1,0:T(8,128)}), f32[128,768]{1,0:T(8,128)}) %reduce-scatter.5.cloned.1.call-update) | async-done | bytes 393232 | tf_op jit(solution)/shard_map/reduce_scatter | solution.py:52
  668.4 65.5 %psum.29 = f32[64,64]{0,1:T(8,128)S(1)} all-reduce(f32[64,64]{0,1:T(8,128)S(1)} %convolution_multiply_fusion.2), channel_id=1, replica_groups=mesh['row'=8,'col'=16] {'row','col'}, use_global_device_ids=true, to_apply=%region_9.10 | all-reduce | flops 4096 | bytes 32768 | tf_op jit(solution)/shard_map/psum | solution.py:86
  739.6 4.9 collective-permute-done.5
  744.6 7.4 collective-permute-done.6
  753.4 17.8 %all_gather.7 = bf16[64,6144]{1,0:T(8,128)(2,1)S(1)} all-gather(bf16[64,768]{1,0:T(8,128)(2,1)S(1)} %get-tuple-element.250), channel_id=1, replica_groups=mesh['row'=8,'col'=16] {'row'}, dimensions={1}, use_global_device_ids=true | all-gather | bytes 884736 | tf_op jit(solution)/shard_map/all_gather | solution.py:22
  780.3 200.0 %while.27 = (s32[]{:T(128)}, f32[64,96,128]{2,0,1:T(8,128)}, f32[64,48,128]{2,0,1:T(8,128)}, s32[]{:T(128)}, s32[576]{0:T(1024)S(1)}, /*index=5*/s32[]{:T(128)},...) while((s32[]{:T(128)}, f32[64,96,128]{2,0,1:T(8,128)}, ...), condition=%wide.region_13.14_spmd.clone, body=%wide.region_10.13_spmd.clone.sunk | while | flops 272632704 | bytes 27274384 | solution.py:51
  786.1 9.1 scatter_fusion.2
  799.7 9.1 scatter_fusion.3
  814.7 9.2 scatter_fusion.2
  828.4 9.2 scatter_fusion.3
  843.4 9.1 scatter_fusion.2
  857.0 9.2 scatter_fusion.3
  872.0 9.1 scatter_fusion.2
  885.6 9.1 scatter_fusion.3
  900.6 9.1 scatter_fusion.2
  914.2 9.1 scatter_fusion.3
  929.1 9.1 scatter_fusion.2
  942.7 9.1 scatter_fusion.3
  957.6 9.1 scatter_fusion.2
  971.2 9.1 scatter_fusion.3
  987.4 79.0 %reduce-scatter.11.cloned.1.call-done = f32[64,768]{1,0:T(8,128)} async-done(((f32[64,6144]{1,0:T(8,128)}), f32[64,768]{1,0:T(8,128)}) %reduce-scatter.11.cloned.1.call-update) | async-done | bytes 196624 | tf_op jit(solution)/shard_map/reduce_scatter | solution.py:55
  1066.4 79.1 %reduce-scatter.9.cloned.1.call-done = f32[64,768]{1,0:T(8,128)} async-done(((f32[64,12288]{1,0:T(8,128)}), f32[64,768]{1,0:T(8,128)}) %reduce-scatter.9.cloned.1.call-update) | async-done | bytes 196624 | tf_op jit(solution)/shard_map/reduce_scatter | solution.py:52
  1148.0 148.0 %all-reduce.3.cloned.1.call-done = (f32[192,192]{1,0:T(8,128)}, f32[192,192]{1,0:T(8,128)}) async-done(((f32[192,192]{1,0:T(8,128)}, f32[192,192]{1,0:T(8,128)}), (f32[192,192]{1,0:T(8,128)}, f32[192,192]{1,0:T(8,128)})) %all-reduce.3.cloned.1.call-update) | async-done | bytes 294928 | tf_op jit(solution)/shard_map/psum | solution.py:94
  (197 shorter events, 179.7 us)
Async XLA Ops:
  7.2 0.9 copy-start
  7.2 125.1 %all-gather.2.cloned.1.call-start = ((), (), s32[]{:S(2)}) async-start(), calls=%async_computation.4 | async-start | bytes 1769472 | tf_op jit(solution)/shard_map/all_gather | solution.py:22
  90.8 16.5 %copy-start.5 = (bf16[128,768]{1,0:T(8,128)(2,1)}, bf16[128,768]{1,0:T(8,128)(2,1)S(1)}, u32[]{:S(2)}) copy-start(bf16[128,768]{1,0:T(8,128)(2,1)S(1)} %pad_maximum_fusion.3) | copy-start | bytes 589828
  90.9 5.6 collective-permute-start
  96.6 10.4 collective-permute-start.1
  107.2 19.8 %copy-start.10 = (s32[1,1,576]{2,1,0:T(1,128)S(1)}, s32[1,1,576]{2,1,0:T(1,128)}, u32[]{:S(2)}) copy-start(s32[1,1,576]{2,1,0:T(1,128)} %param.12) | copy-start | bytes 6916
  107.2 19.9 %copy-start.11 = (s32[1,1,576]{2,1,0:T(1,128)S(1)}, s32[1,1,576]{2,1,0:T(1,128)}, u32[]{:S(2)}) copy-start(s32[1,1,576]{2,1,0:T(1,128)} %param.13) | copy-start | bytes 6916
  107.2 16.4 %collective-permute-start.2 = (bf16[128,3072]{1,0:T(8,128)(2,1)S(1)}, bf16[128,3072]{1,0:T(8,128)(2,1)S(1)}, u32[]{:S(2)}, u32[]{:S(2)}) collective-permute-start(bf16[128,3072]{1,0:T(8,128)(2,1)S(1)} %maximum_select_fusion.5), channel_id=1, source_target_pairs={{0,4},{1,5},{2,6},{3,7},{4,0},{5,1},{6,2},{7,3},{8,12},{9,13},{10,... | collective-permute-start | bytes 2359304 | tf_op jit(solution)/shard_map/ppermute | solution.py:17
  107.4 19.5 %copy-start.6 = (bf16[128,768]{1,0:T(8,128)(2,1)S(1)}, bf16[128,768]{1,0:T(8,128)(2,1)}, u32[]{:S(2)}) copy-start(bf16[128,768]{1,0:T(8,128)(2,1)} %copy-done.5) | copy-start | bytes 589828
  107.4 473.8 %reduce-scatter.7.cloned.1.call-start = ((), (), s32[]{:S(2)}) async-start(), calls=%async_computation.6 | async-start | bytes 3538944 | tf_op jit(solution)/shard_map/reduce_scatter | solution.py:55
  125.2 34.1 %collective-permute-start.3 = (bf16[128,6144]{1,0:T(8,128)(2,1)}, bf16[128,6144]{1,0:T(8,128)(2,1)}, u32[]{:S(2)}, u32[]{:S(2)}) collective-permute-start(bf16[128,6144]{1,0:T(8,128)(2,1)} %maximum_select_fusion.2), channel_id=1, source_target_pairs={{0,8},{1,9},{2,10},{3,11},{4,12},{5,13},{6,14},{7,15},{8,0},{9,1},... | collective-permute-start | bytes 4718600 | tf_op jit(solution)/shard_map/ppermute | solution.py:17
  464.8 202.0 %reduce-scatter.5.cloned.1.call-start = ((), (), s32[]{:S(2)}) async-start(), calls=%async_computation.5 | async-start | bytes 6684672 | tf_op jit(solution)/shard_map/reduce_scatter | solution.py:52
  471.0 595.5 %reduce-scatter.11.cloned.1.call-start = ((), (), s32[]{:S(2)}) async-start(), calls=%async_computation.8 | async-start | bytes 1769472 | tf_op jit(solution)/shard_map/reduce_scatter | solution.py:55
  668.0 103.1 %copy-start.3 = (f32[128,768]{1,0:T(8,128)}, f32[128,768]{1,0:T(8,128)S(1)}, u32[]{:S(2)}) copy-start(f32[128,768]{1,0:T(8,128)S(1)} %add.116) | copy-start | bytes 1179652
  734.8 3.5 collective-permute-start.4
  738.3 6.1 collective-permute-start.5
  744.5 7.5 collective-permute-start.6
  752.2 21.2 %collective-permute-start.7 = (bf16[64,6144]{1,0:T(8,128)(2,1)S(1)}, bf16[64,6144]{1,0:T(8,128)(2,1)}, u32[]{:S(2)}, u32[]{:S(2)}) collective-permute-start(bf16[64,6144]{1,0:T(8,128)(2,1)S(1)} %maximum_select_fusion.7), channel_id=1, source_target_pairs={{0,8},{1,9},{2,10},{3,11},{4,12},{5,13},{6,14},{7,15},{8,0},{9,1},... | collective-permute-start | bytes 2359304 | tf_op jit(solution)/shard_map/ppermute | solution.py:17
  980.3 2.9 copy-start.2
  983.1 162.4 %reduce-scatter.9.cloned.1.call-start = ((), (), s32[]{:S(2)}) async-start(), calls=%async_computation.7 | async-start | bytes 3342336 | tf_op jit(solution)/shard_map/reduce_scatter | solution.py:52
  985.0 0.9 copy-start.7
  985.0 1.0 copy-start.8
  985.0 2.3 copy-start.4
  985.1 310.9 %all-reduce.3.cloned.1.call-start = ((), (), s32[]{:S(2)}) async-start(), calls=%async_computation.9 | async-start | bytes 786432 | tf_op jit(solution)/shard_map/psum | solution.py:94
  986.1 313.2 %copy-start.1 = (f32[64,768]{1,0:T(8,128)S(1)}, f32[64,768]{1,0:T(8,128)}, u32[]{:S(2)}) copy-start(f32[64,768]{1,0:T(8,128)} %param.10) | copy-start | bytes 589828
  1146.6 152.6 %copy-start.9 = (f32[64,768]{1,0:T(8,128)}, f32[64,768]{1,0:T(8,128)S(1)}, u32[]{:S(2)}) copy-start(f32[64,768]{1,0:T(8,128)S(1)} %add.117) | copy-start | bytes 589828
Sparse Core Ops, SparseCore 0:
  107.5 24.7 all-gather.1
  465.0 116.2 reduce-scatter.6
  584.7 82.1 reduce-scatter.4
  983.3 83.1 reduce-scatter.10
  1069.6 75.8 reduce-scatter.8
  1150.8 145.1 all-reduce.2
